TPU v7x, 512 devices: a whole 4x8x8 slice. The times are simulated.
512 devices in a mesh: ctx: 64 (over x, z, y_hi), ch: 8 (over y_lo, core).
Axes of the slice: x: 4, y: 8 (y_hi: 2, y_lo: 4; y = y_hi * 4 + y_lo), z: 8, core: 2. Of those that a mesh axis runs over, the one named last changes fastest.
Arguments:
- outer_gate: bfloat16 [8192, 4096], P('ctx', 'ch'), may hold values from -6 to 6
- inner_gate: bfloat16 [8192, 4096], P('ctx', 'ch'), may hold values from -6 to 6
- value_path: bfloat16 [8192, 4096], P('ctx', 'ch'), may hold values from -6 to 6
- long_filter: float32 [8192, 4096], P('ctx', 'ch'), may hold values from -0.0625 to 0.0625
- skip_gain: float32 [4096], P('ch'), may hold values from 0.25 to 1.75
- cotangent: bfloat16 [8192, 4096], P('ctx', 'ch'), may hold values from -32 to 32
Outputs:
- hyena_out: bfloat16 [8192, 4096], P('ctx', 'ch')
- grad_outer: bfloat16 [8192, 4096], P('ctx', 'ch')
- grad_inner: bfloat16 [8192, 4096], P('ctx', 'ch')
- grad_value: bfloat16 [8192, 4096], P('ctx', 'ch')
- grad_filter: float32 [8192, 4096], P('ctx', 'ch')
All inputs are finite; a program needn't handle non-finite values.
Results may differ from a plain program's by a relative error of at most 0.001.
Values may be sent and summed in bfloat16 or wider, within the bound.
A program may use at most 64 MiB of HBM per device.

v0:
```python
import functools

import jax
import jax.numpy as jnp
import numpy as np
from jax import lax
from jax.experimental import pallas as pl
from jax.experimental.pallas import tpu as pltpu
from jax.sharding import PartitionSpec as P

F32 = jnp.float32
BF16 = jnp.bfloat16
MESH = pl.DeviceIdType.MESH

NCTX = 64
NCH = 8
BLK = 128
LANES = 512
NAR = LANES // NCTX
ROWS = 3 * NAR


def split(x):
    hi = x.astype(BF16)
    lo = (x - hi.astype(F32)).astype(BF16)
    return hi, lo


def tables():
    total = NCTX * BLK
    p = np.arange(NCTX)
    s = np.arange(BLK)
    k = np.arange(NCTX) + 0.25
    a1 = 2 * np.pi * np.outer(k, p) / NCTX
    w1 = np.concatenate([np.cos(a1), -np.sin(a1)], axis=0)
    at = 2 * np.pi * np.outer(k, s) / total
    tw = np.stack([np.cos(at), -np.sin(at)])
    a2 = 2 * np.pi * (np.outer(s, s) % BLK) / BLK
    c, sn = np.cos(a2), np.sin(a2)
    w2 = np.block([[c, -sn], [sn, c]])

    def parts(m):
        hi = m.astype(BF16)
        lo = (m - hi.astype(np.float64)).astype(BF16)
        return hi, lo

    w1h, w1l = parts(w1)
    w1f = np.concatenate([w1h, w1l, w1h], axis=1)
    w1i = np.concatenate([w1h.T, w1l.T, w1h.T], axis=1)
    w2h, w2l = parts(w2)
    w2f = np.stack([w2h, w2l])
    w2i = np.stack([w2h.T, w2l.T])
    return w1f, w1i, tw.astype(np.float32), w2f, w2i


def dot(a, b):
    return jnp.dot(a, b, preferred_element_type=F32)


def dot3(x, w_ref):
    hi, lo = split(x)
    wh = w_ref[0]
    return dot(hi, wh) + (dot(hi, w_ref[1]) + dot(lo, wh))


def conv_kernel(
    outer, inner, value, cot, filt, w1f, w1i, tw, w2f, w2i,
    back, sums,
    send, recv, ret, part, chbuf,
    send_sem, recv_sem, send2_sem, recv2_sem, sq_send, sq_recv, loc_sem, sqx_send, sqx_recv,
):
    me = lax.axis_index("ctx")
    ch = lax.axis_index("ch")

    barrier = pltpu.get_barrier_semaphore()

    def greet(i, _):
        pl.semaphore_signal(
            barrier, inc=1, device_id={"ctx": lax.rem(me + i, NCTX)}, device_id_type=MESH
        )
        return 0

    lax.fori_loop(1, NCTX, greet, 0)
    for j in range(1, NCH):
        pl.semaphore_signal(
            barrier, inc=1, device_id={"ch": lax.rem(ch + j, NCH)}, device_id_type=MESH
        )

    mixed = inner[...].astype(F32) * value[...].astype(F32)
    send[:, 0:NAR, :] = mixed.T.reshape(NCTX, NAR, BLK)
    gconv = cot[...].astype(F32) * outer[...].astype(F32)
    send[:, NAR : 2 * NAR, :] = gconv.T.reshape(NCTX, NAR, BLK)
    send[:, 2 * NAR : 3 * NAR, :] = filt[...].T.reshape(NCTX, NAR, BLK)

    pl.semaphore_wait(barrier, NCTX - 1 + NCH - 1)

    own = pltpu.make_async_copy(send.at[me], recv.at[pl.ds(me * ROWS, ROWS)], recv_sem)
    own.start()

    def scatter(i, _):
        to = lax.rem(me + i, NCTX)
        pltpu.make_async_remote_copy(
            src_ref=send.at[to],
            dst_ref=recv.at[pl.ds(me * ROWS, ROWS)],
            send_sem=send_sem,
            recv_sem=recv_sem,
            device_id={"ctx": to},
            device_id_type=MESH,
        ).start()
        return 0

    lax.fori_loop(1, NCTX, scatter, 0)
    pltpu.make_async_copy(recv, recv, recv_sem).wait()

    tr, ti = tw[0], tw[1]
    wa, wb = w1f[...], w1i[...]

    def forward(sig, c):
        x = recv[pl.ds(sig * NAR + c, NCTX, stride=ROWS), :]
        hi, lo = split(x)
        z = dot(wa, jnp.concatenate([hi, hi, lo], axis=0))
        zr, zi = z[:NCTX], z[NCTX:]
        return jnp.concatenate([zr * tr - zi * ti, zr * ti + zi * tr], axis=1)

    def inverse(v):
        vr, vi = v[:, :BLK], v[:, BLK:]
        u = jnp.concatenate([vr * tr + vi * ti, vi * tr - vr * ti], axis=0)
        hi, lo = split(u)
        return dot(wb, jnp.concatenate([hi, hi, lo], axis=0)) * (1.0 / (NCTX * BLK))

    def channel(c, acc):
        u = jnp.concatenate([forward(0, c), forward(1, c), forward(2, c)], axis=0)
        x = dot3(u, w2f)
        m, g, f = x[:NCTX], x[NCTX : 2 * NCTX], x[2 * NCTX :]
        mr, mi = m[:, :BLK], m[:, BLK:]
        gr, gi = g[:, :BLK], g[:, BLK:]
        fr, fi = f[:, :BLK], f[:, BLK:]
        y = jnp.concatenate(
            [
                jnp.concatenate([fr * mr - fi * mi, fr * mi + fi * mr], axis=1),
                jnp.concatenate([fr * gr + fi * gi, fr * gi - fi * gr], axis=1),
                jnp.concatenate([mr * gr + mi * gi, mr * gi - mi * gr], axis=1),
            ],
            axis=0,
        )
        v = dot3(y, w2i)
        ret[pl.ds(c, NCTX, stride=ROWS), :] = inverse(v[:NCTX])
        ret[pl.ds(NAR + c, NCTX, stride=ROWS), :] = inverse(v[NCTX : 2 * NCTX])
        lag = inverse(v[2 * NCTX :])
        ret[pl.ds(2 * NAR + c, NCTX, stride=ROWS), :] = lag
        sq = lag * lag
        return acc + jnp.sum(sq.reshape(NCTX // 8, 8, BLK), axis=0)

    acc = lax.fori_loop(0, NAR, channel, jnp.zeros((8, BLK), F32))

    part[...] = acc
    chbuf[ch] = acc
    for j in range(1, NCH):
        pltpu.make_async_remote_copy(
            src_ref=part,
            dst_ref=chbuf.at[ch],
            send_sem=sq_send,
            recv_sem=sq_recv,
            device_id={"ch": lax.rem(ch + j, NCH)},
            device_id_type=MESH,
        ).start()

    own2 = pltpu.make_async_copy(ret.at[pl.ds(me * ROWS, ROWS)], back.at[me], recv2_sem)
    own2.start()

    def gather(i, _):
        to = lax.rem(me + i, NCTX)
        pltpu.make_async_remote_copy(
            src_ref=ret.at[pl.ds(to * ROWS, ROWS)],
            dst_ref=back.at[me],
            send_sem=send2_sem,
            recv_sem=recv2_sem,
            device_id={"ctx": to},
            device_id_type=MESH,
        ).start()
        return 0

    lax.fori_loop(1, NCTX, gather, 0)

    pltpu.make_async_copy(chbuf.at[pl.ds(0, NCH - 1)], chbuf.at[pl.ds(0, NCH - 1)], sq_send).wait()
    pltpu.make_async_copy(chbuf.at[pl.ds(0, NCH - 1)], chbuf.at[pl.ds(0, NCH - 1)], sq_recv).wait()
    group = jnp.sum(jnp.sum(chbuf[...], axis=0), axis=0, keepdims=True)
    part[0:1, :] = group
    sums[me] = group

    def spread(i, _):
        to = lax.rem(me + i, NCTX)
        pltpu.make_async_remote_copy(
            src_ref=part.at[pl.ds(0, 1)],
            dst_ref=sums.at[me],
            send_sem=sqx_send,
            recv_sem=sqx_recv,
            device_id={"ctx": to},
            device_id_type=MESH,
        ).start()
        return 0

    lax.fori_loop(1, NCTX, spread, 0)

    rest = pl.ds(0, (NCTX - 1) * ROWS)
    pltpu.make_async_copy(recv.at[rest], recv.at[rest], send_sem).wait()
    pltpu.make_async_copy(ret.at[rest], ret.at[rest], send2_sem).wait()
    others = pl.ds(0, NCTX - 1)
    pltpu.make_async_copy(sums.at[others], sums.at[others], sqx_send).wait()
    pltpu.make_async_copy(sums.at[others], sums.at[others], sqx_recv).wait()
    pltpu.make_async_copy(back, back, recv2_sem).wait()


def gate_kernel(
    outer, inner, value, cot, skip, back, sums, hyena, gouter, ginner, gvalue, gfilter
):
    inner_f = inner[...].astype(F32)
    value_f = value[...].astype(F32)
    outer_f = outer[...].astype(F32)
    cot_f = cot[...].astype(F32)
    gain = skip[...]
    conv = back[:, 0:NAR, :].reshape(LANES, BLK).T
    base = conv + gain * (inner_f * value_f)
    hyena[...] = (outer_f * base).astype(BF16)
    gouter[...] = (cot_f * base).astype(BF16)
    gmixed = back[:, NAR : 2 * NAR, :].reshape(LANES, BLK).T + gain * (cot_f * outer_f)
    ginner[...] = (gmixed * value_f).astype(BF16)
    gvalue[...] = (gmixed * inner_f).astype(BF16)
    squares = jnp.sum(jnp.sum(sums[...], axis=0), axis=1, keepdims=True)
    limit = float(NCTX * BLK) * float(np.sqrt(LANES * NCH))
    scale = jnp.minimum(1.0, limit / jnp.sqrt(squares + 1e-06))
    gfilter[...] = back[:, 2 * NAR :, :].reshape(LANES, BLK).T * scale


def local(outer_gate, inner_gate, value_path, long_filter, skip_gain, cotangent):
    vmem = pl.BlockSpec(memory_space=pltpu.VMEM)
    consts = tables()
    back, sums = pl.pallas_call(
        conv_kernel,
        out_shape=(
            jax.ShapeDtypeStruct((NCTX, ROWS, BLK), F32),
            jax.ShapeDtypeStruct((NCTX, 1, BLK), F32),
        ),
        in_specs=[vmem] * 10,
        out_specs=(vmem, vmem),
        scratch_shapes=[
            pltpu.VMEM((NCTX, ROWS, BLK), F32),
            pltpu.VMEM((NCTX * ROWS, BLK), F32),
            pltpu.VMEM((NCTX * ROWS, BLK), F32),
            pltpu.VMEM((8, BLK), F32),
            pltpu.VMEM((NCH, 8, BLK), F32),
        ]
        + [pltpu.SemaphoreType.DMA] * 9,
        compiler_params=pltpu.CompilerParams(
            collective_id=0, has_side_effects=True, vmem_limit_bytes=32 * 1024 * 1024
        ),
    )(outer_gate, inner_gate, value_path, cotangent, long_filter, *consts)
    arr = jax.ShapeDtypeStruct((BLK, LANES), BF16)
    return pl.pallas_call(
        gate_kernel,
        out_shape=(arr, arr, arr, arr, jax.ShapeDtypeStruct((BLK, LANES), F32)),
        in_specs=[vmem] * 7,
        out_specs=(vmem,) * 5,
        compiler_params=pltpu.CompilerParams(vmem_limit_bytes=32 * 1024 * 1024),
    )(outer_gate, inner_gate, value_path, cotangent, skip_gain.reshape(1, LANES), back, sums)


def solution(mesh):
    big = P("ctx", "ch")
    return jax.shard_map(
        local,
        mesh=mesh,
        in_specs=(big, big, big, big, P("ch"), big),
        out_specs=(big,) * 5,
        check_vma=False,
    )
```

profile of v0, /device:TPU:1, one launch (start us, length us, event | category | flops | bytes accessed | tf_op | source)
XLA Modules:
  0.0 86.3 jit_solution(18125103781860631855)
XLA Ops:
  0.6 0.0 copy-start
  0.6 0.9 %copy-done = bf16[128,512]{1,0:T(8,128)(2,1)S(1)} copy-done((bf16[128,512]{1,0:T(8,128)(2,1)S(1)}, bf16[128,512]{1,0:T(8,128)(2,1)}, u32[]{:S(2)}) %copy-start) | copy-done | bytes 131096
  1.5 0.0 copy-start.1
  1.5 0.9 %copy-done.1 = bf16[128,512]{1,0:T(8,128)(2,1)S(1)} copy-done((bf16[128,512]{1,0:T(8,128)(2,1)S(1)}, bf16[128,512]{1,0:T(8,128)(2,1)}, u32[]{:S(2)}) %copy-start.1) | copy-done | bytes 131096
  2.4 0.0 copy-start.2
  2.4 0.9 %copy-done.2 = bf16[128,512]{1,0:T(8,128)(2,1)S(1)} copy-done((bf16[128,512]{1,0:T(8,128)(2,1)S(1)}, bf16[128,512]{1,0:T(8,128)(2,1)}, u32[]{:S(2)}) %copy-start.2) | copy-done | bytes 131096
  3.3 0.0 copy-start.3
  3.3 0.9 %copy-done.3 = bf16[128,512]{1,0:T(8,128)(2,1)S(1)} copy-done((bf16[128,512]{1,0:T(8,128)(2,1)S(1)}, bf16[128,512]{1,0:T(8,128)(2,1)}, u32[]{:S(2)}) %copy-start.3) | copy-done | bytes 131096
  4.3 0.0 copy-start.4
  4.3 0.9 %copy-done.4 = f32[128,512]{1,0:T(8,128)S(1)} copy-done((f32[128,512]{1,0:T(8,128)S(1)}, f32[128,512]{1,0:T(8,128)}, u32[]{:S(2)}) %copy-start.4) | copy-done | bytes 262168
  5.2 0.0 copy-start.5
  5.2 0.9 %copy-done.5 = bf16[2,256,256]{2,1,0:T(8,128)(2,1)S(1)} copy-done((bf16[2,256,256]{2,1,0:T(8,128)(2,1)S(1)}, bf16[2,256,256]{2,1,0:T(8,128)(2,1)}, u32[]{:S(2)}) %copy-start.5) | copy-done | bytes 262168
  6.2 0.0 copy-start.6
  6.2 0.9 %copy-done.6 = bf16[2,256,256]{2,1,0:T(8,128)(2,1)S(1)} copy-done((bf16[2,256,256]{2,1,0:T(8,128)(2,1)S(1)}, bf16[2,256,256]{2,1,0:T(8,128)(2,1)}, u32[]{:S(2)}) %copy-start.6) | copy-done | bytes 262168
  7.1 0.0 copy-start.7
  7.1 0.8 copy-done.7
  7.9 0.0 copy-start.8
  7.9 0.8 copy-done.8
  8.8 0.0 copy-start.9
  8.8 0.8 copy-done.9
  9.6 74.9 %shard_map.146 = (f32[64,24,128]{2,1,0:T(8,128)S(1)}, f32[64,1,128]{2,1,0:T(1,128)S(1)}) custom-call(bf16[128,512]{1,0:T(8,128)(2,1)S(1)} %copy-done, bf16[128,512]{1,0:T(8,128)(2,1)S(1)} %copy-done.1, bf16[128,512]{1,0:T(8,128)(2,1)S(1)} %copy-done.2, bf16[128,512]{1,0:T(8,128)(2,1)S(1)} %copy-done.3, f32[128,512]{1,0:T(8,128)S(1)} %copy-done.4, ...), custom_call_target="tpu_custom_call" | custom-call | tf_op jit(solution)/shard_map/pallas_call | solution.py:238
  84.5 0.0 copy-start.10
  84.5 0.7 copy-done.10
  85.2 1.1 %shard_map.147 = (bf16[128,512]{1,0:T(8,128)(2,1)}, bf16[128,512]{1,0:T(8,128)(2,1)}, bf16[128,512]{1,0:T(8,128)(2,1)}, bf16[128,512]{1,0:T(8,128)(2,1)}, f32[128,512]{1,0:T(8,128)}) custom-call(bf16[128,512]{1,0:T(8,128)(2,1)S(1)} %copy-done, bf16[128,512]{1,0:T(8,128)(2,1)S(1)} %copy-done.1, bf16[128,512]{1,0:T(8,128)(2,1)S(1)} %copy-done.2, ...), custom_call_target="tpu_custom_call" | custom-call | tf_op jit(solution)/shard_map/pallas_call | solution.py:259
Async XLA Ops:
  0.6 0.9 %copy-start = (bf16[128,512]{1,0:T(8,128)(2,1)S(1)}, bf16[128,512]{1,0:T(8,128)(2,1)}, u32[]{:S(2)}) copy-start(bf16[128,512]{1,0:T(8,128)(2,1)} %outer.3) | copy-start | bytes 393220
  1.5 0.9 %copy-start.1 = (bf16[128,512]{1,0:T(8,128)(2,1)S(1)}, bf16[128,512]{1,0:T(8,128)(2,1)}, u32[]{:S(2)}) copy-start(bf16[128,512]{1,0:T(8,128)(2,1)} %inner.3) | copy-start | bytes 393220
  2.4 0.9 %copy-start.2 = (bf16[128,512]{1,0:T(8,128)(2,1)S(1)}, bf16[128,512]{1,0:T(8,128)(2,1)}, u32[]{:S(2)}) copy-start(bf16[128,512]{1,0:T(8,128)(2,1)} %value.3) | copy-start | bytes 393220
  3.3 0.9 %copy-start.3 = (bf16[128,512]{1,0:T(8,128)(2,1)S(1)}, bf16[128,512]{1,0:T(8,128)(2,1)}, u32[]{:S(2)}) copy-start(bf16[128,512]{1,0:T(8,128)(2,1)} %cot.3) | copy-start | bytes 393220
  4.3 0.9 %copy-start.4 = (f32[128,512]{1,0:T(8,128)S(1)}, f32[128,512]{1,0:T(8,128)}, u32[]{:S(2)}) copy-start(f32[128,512]{1,0:T(8,128)} %filt.1) | copy-start | bytes 786436
  5.2 0.9 %copy-start.5 = (bf16[2,256,256]{2,1,0:T(8,128)(2,1)S(1)}, bf16[2,256,256]{2,1,0:T(8,128)(2,1)}, u32[]{:S(2)}) copy-start(bf16[2,256,256]{2,1,0:T(8,128)(2,1)} %constant.14.clone.w2i) | copy-start | bytes 786436
  6.2 0.9 %copy-start.6 = (bf16[2,256,256]{2,1,0:T(8,128)(2,1)S(1)}, bf16[2,256,256]{2,1,0:T(8,128)(2,1)}, u32[]{:S(2)}) copy-start(bf16[2,256,256]{2,1,0:T(8,128)(2,1)} %constant.13.clone.w2f) | copy-start | bytes 786436
  7.1 0.8 copy-start.7
  7.9 0.8 copy-start.8
  8.8 0.8 copy-start.9
  84.5 0.7 copy-start.10
where the time goes:
time: 86.7 us; the launch traced here: 86.3 us
  Pallas kernels  76 us (88%)
  local copies, waits for them, and re-layouts  9.61 us (11%)
    pallas_call x1, Pallas kernels, local(): pl.pallas_call(conv_kernel, out_shape=(jax.ShapeDtypeStruct((NCTX, ROWS,...  74.9 us
    unnamed x22, local copies, waits for them, and re-layouts  9.61 us

commit v1 on v0

v1 whole, which is shorter than its diff:
```python
import jax
import jax.numpy as jnp
import numpy as np
from jax import lax
from jax.experimental import pallas as pl
from jax.experimental.pallas import tpu as pltpu
from jax.sharding import PartitionSpec as P

F32 = jnp.float32
BF16 = jnp.bfloat16
MESH = pl.DeviceIdType.MESH

NCTX = 64
NCH = 8
VMEM_LIMIT = 60 * 1024 * 1024
BLK = 128
LANES = 512
NAR = LANES // NCTX


def split(x):
    hi = x.astype(BF16)
    lo = (x - hi.astype(F32)).astype(BF16)
    return hi, lo


def tables():
    total = NCTX * BLK
    p = np.arange(NCTX)
    s = np.arange(BLK)
    k = np.arange(NCTX) + 0.25
    a1 = 2 * np.pi * np.outer(k, p) / NCTX
    w1 = np.concatenate([np.cos(a1), -np.sin(a1)], axis=0)
    at = 2 * np.pi * np.outer(k, s) / total
    tw = np.stack([np.cos(at), -np.sin(at)])
    a2 = 2 * np.pi * (np.outer(s, s) % BLK) / BLK
    c, sn = np.cos(a2), np.sin(a2)
    w2 = np.block([[c, -sn], [sn, c]])

    def parts(m):
        hi = m.astype(BF16)
        lo = (m - hi.astype(np.float64)).astype(BF16)
        return hi, lo

    w1h, w1l = parts(w1)
    w1f = np.concatenate([w1h, w1l, w1h], axis=1)
    w1i = np.concatenate([w1h.T, w1l.T, w1h.T], axis=1)
    w2h, w2l = parts(w2)
    w2f = np.stack([w2h, w2l])
    w2i = np.stack([w2h.T, w2l.T])
    return w1f, w1i, tw.astype(np.float32), w2f, w2i


def dot(a, b):
    return jnp.dot(a, b, preferred_element_type=F32)


def dot3(x, w_ref):
    hi, lo = split(x)
    wh = w_ref[0]
    return dot(hi, wh) + (dot(hi, w_ref[1]) + dot(lo, wh))


def place(me):
    return lax.div(me, 16), lax.rem(lax.div(me, 2), 8), lax.rem(me, 2)


def peer(me, i):
    x, z, y = place(me)
    k, j = lax.div(i, 8), lax.rem(i, 8)
    dy = 1 - lax.div(k, 4)
    k = lax.rem(k, 4)
    dx = 2 + lax.div(k + 1, 2) * (1 - 2 * lax.rem(k, 2))
    dz = 4 + lax.div(j + 1, 2) * (1 - 2 * lax.rem(j, 2))
    return lax.rem(x + dx, 4) * 16 + lax.rem(z + dz, 8) * 2 + lax.rem(y + dy, 2)


def conv_kernel(
    outer_h, inner_h, value_h, cot_h, filt_h, w1f_h, w1i_h, tw_h, w2f_h, w2i_h,
    back, back_lag, total,
    outer, inner, value, cot, filt, w1f, w1i, tw, w2f, w2i,
    send, send_f, recv, recv_f, ret, ret_lag, spec, part, sums,
    load_sem, send_sem, recv_sem, sendf_sem, recvf_sem, sendl_sem, recvl_sem,
    sendr_sem, recvr_sem, sq_send, sq_recv, own_sem,
):
    me = lax.axis_index("ctx")
    ch = lax.axis_index("ch")
    x, z, y = place(me)

    loads = [
        pltpu.make_async_copy(src, dst, load_sem.at[n])
        for n, (src, dst) in enumerate(
            [
                (inner_h, inner), (value_h, value), (cot_h, cot), (outer_h, outer),
                (filt_h, filt), (w1f_h, w1f), (w1i_h, w1i), (tw_h, tw), (w2f_h, w2f),
                (w2i_h, w2i),
            ]
        )
    ]
    for load in loads:
        load.start()

    barrier = pltpu.get_barrier_semaphore()

    def greet(i, _):
        pl.semaphore_signal(
            barrier, inc=1, device_id={"ctx": peer(me, i)}, device_id_type=MESH
        )
        return 0

    lax.fori_loop(0, NCTX - 1, greet, 0)
    for j in range(1, NCH):
        pl.semaphore_signal(
            barrier, inc=1, device_id={"ch": lax.rem(ch + j, NCH)}, device_id_type=MESH
        )

    for load in loads[:5]:
        load.wait()
    mixed = inner[...].astype(F32) * value[...].astype(F32)
    send[:, 0:NAR, :] = mixed.T.reshape(NCTX, NAR, BLK)
    gconv = cot[...].astype(F32) * outer[...].astype(F32)
    send[:, NAR : 2 * NAR, :] = gconv.T.reshape(NCTX, NAR, BLK)
    send_f[...] = filt[...].T.reshape(NCTX, NAR, BLK)
    for load in loads[5:]:
        load.wait()

    pl.semaphore_wait(barrier, NCTX - 1 + NCH - 1)

    def spread(src, dst, send_s, recv_s):
        def one(i, _):
            to = peer(me, i)
            pltpu.make_async_remote_copy(
                src_ref=src(to),
                dst_ref=dst(me),
                send_sem=send_s,
                recv_sem=recv_s,
                device_id={"ctx": to},
                device_id_type=MESH,
            ).start()
            return 0

        lax.fori_loop(0, NCTX - 1, one, 0)
        pltpu.make_async_copy(src(me), dst(me), recv_s).start()

    spread(lambda d: send.at[d], lambda d: recv.at[pl.ds(d * 16, 16)], send_sem, recv_sem)
    spread(lambda d: send_f.at[d], lambda d: recv_f.at[pl.ds(d * 8, 8)], sendf_sem, recvf_sem)

    tr, ti = tw[0], tw[1]
    wa, wb = w1f[...], w1i[...]

    def forward(rows):
        hi, lo = split(rows)
        z = dot(wa, jnp.concatenate([hi, hi, lo], axis=0))
        zr, zi = z[:NCTX], z[NCTX:]
        return jnp.concatenate([zr * tr - zi * ti, zr * ti + zi * tr], axis=1)

    def inverse(v):
        vr, vi = v[:, :BLK], v[:, BLK:]
        u = jnp.concatenate([vr * tr + vi * ti, vi * tr - vr * ti], axis=0)
        hi, lo = split(u)
        return dot(wb, jnp.concatenate([hi, hi, lo], axis=0)) * (1.0 / (NCTX * BLK))

    def correlate(a, b):
        ar, ai, br, bi = a[:, :BLK], a[:, BLK:], b[:, :BLK], b[:, BLK:]
        return jnp.concatenate([ar * br + ai * bi, ar * bi - ai * br], axis=1)

    def convolve(a, b):
        ar, ai, br, bi = a[:, :BLK], a[:, BLK:], b[:, :BLK], b[:, BLK:]
        return jnp.concatenate([ar * br - ai * bi, ar * bi + ai * br], axis=1)

    def pieces(v):
        return [v[n * NCTX : (n + 1) * NCTX] for n in range(v.shape[0] // NCTX)]

    def lag_pair(n, acc):
        c = 2 * n
        u = [forward(recv[pl.ds(c + d, NCTX, stride=16), :]) for d in (0, 1, NAR, NAR + 1)]
        f = dot3(jnp.concatenate(u, axis=0), w2f)
        spec[n] = f
        m0, m1, g0, g1 = pieces(f)
        v = dot3(jnp.concatenate([correlate(m0, g0), correlate(m1, g1)], axis=0), w2i)
        for d, part_v in enumerate(pieces(v)):
            lag = inverse(part_v)
            ret_lag[pl.ds(c + d, NCTX, stride=8), :] = lag
            acc = acc + jnp.sum((lag * lag).reshape(NCTX // 8, 8, BLK), axis=0)
        return acc

    def conv_pair(n, carry):
        c = 2 * n
        u = [forward(recv_f[pl.ds(c + d, NCTX, stride=8), :]) for d in (0, 1)]
        f0, f1 = pieces(dot3(jnp.concatenate(u, axis=0), w2f))
        m0, m1, g0, g1 = pieces(spec[n])
        v = dot3(
            jnp.concatenate(
                [convolve(f0, m0), convolve(f1, m1), correlate(f0, g0), correlate(f1, g1)],
                axis=0,
            ),
            w2i,
        )
        for d, part_v in zip((0, 1, NAR, NAR + 1), pieces(v)):
            ret[pl.ds(c + d, NCTX, stride=16), :] = inverse(part_v)
        return carry

    def share(stage, mine, value, device):
        part[stage] = value
        sums[stage, mine] = value
        for j in range(1, 8):
            pltpu.make_async_remote_copy(
                src_ref=part.at[stage],
                dst_ref=sums.at[stage, mine],
                send_sem=sq_send.at[stage],
                recv_sem=sq_recv.at[stage],
                device_id=device(lax.rem(mine + j, 8)),
                device_id_type=MESH,
            ).start()

    def gathered(stage):
        seven = sums.at[stage, pl.ds(0, 7)]
        pltpu.make_async_copy(seven, seven, sq_send.at[stage]).wait()
        pltpu.make_async_copy(seven, seven, sq_recv.at[stage]).wait()
        return jnp.sum(sums[stage], axis=0)

    pltpu.make_async_copy(recv, recv, recv_sem).wait()
    acc = lax.fori_loop(0, NAR // 2, lag_pair, jnp.zeros((8, BLK), F32))
    share(0, ch, acc, lambda k: {"ch": k})
    spread(lambda d: ret_lag.at[pl.ds(d * 8, 8)], lambda d: back_lag.at[d], sendl_sem, recvl_sem)

    pltpu.make_async_copy(recv_f, recv_f, recvf_sem).wait()
    lax.fori_loop(0, 2, conv_pair, 0)
    share(1, z, gathered(0), lambda k: {"ctx": x * 16 + k * 2 + y})
    lax.fori_loop(2, 4, conv_pair, 0)
    share(2, x * 2 + y, gathered(1), lambda k: {"ctx": lax.div(k, 2) * 16 + z * 2 + lax.rem(k, 2)})
    spread(lambda d: ret.at[pl.ds(d * 16, 16)], lambda d: back.at[d], sendr_sem, recvr_sem)
    total[...] = gathered(2)

    others = pl.ds(0, (NCTX - 1) * 16)
    pltpu.make_async_copy(recv.at[others], recv.at[others], send_sem).wait()
    pltpu.make_async_copy(ret.at[others], ret.at[others], sendr_sem).wait()
    others = pl.ds(0, (NCTX - 1) * 8)
    pltpu.make_async_copy(recv_f.at[others], recv_f.at[others], sendf_sem).wait()
    pltpu.make_async_copy(ret_lag.at[others], ret_lag.at[others], sendl_sem).wait()
    pltpu.make_async_copy(back_lag, back_lag, recvl_sem).wait()
    pltpu.make_async_copy(back, back, recvr_sem).wait()


def gate_kernel(
    outer_h, inner_h, value_h, cot_h, skip, back_h, lag_h, total,
    hyena, gouter, ginner, gvalue, gfilter,
    outer, inner, value, cot, back, back_lag, sem,
):
    loads = [
        pltpu.make_async_copy(src, dst, sem.at[n])
        for n, (src, dst) in enumerate(
            [
                (back_h, back), (inner_h, inner), (value_h, value), (outer_h, outer),
                (cot_h, cot), (lag_h, back_lag),
            ]
        )
    ]
    for load in loads:
        load.start()
    for load in loads:
        load.wait()
    inner_f = inner[...].astype(F32)
    value_f = value[...].astype(F32)
    outer_f = outer[...].astype(F32)
    cot_f = cot[...].astype(F32)
    gain = skip[...]
    conv = back[:, 0:NAR, :].reshape(LANES, BLK).T
    base = conv + gain * (inner_f * value_f)
    hyena[...] = (outer_f * base).astype(BF16)
    gouter[...] = (cot_f * base).astype(BF16)
    gmixed = back[:, NAR : 2 * NAR, :].reshape(LANES, BLK).T + gain * (cot_f * outer_f)
    ginner[...] = (gmixed * value_f).astype(BF16)
    gvalue[...] = (gmixed * inner_f).astype(BF16)
    squares = jnp.sum(jnp.sum(total[...], axis=0, keepdims=True), axis=1, keepdims=True)
    limit = float(NCTX * BLK) * float(np.sqrt(LANES * NCH))
    scale = jnp.minimum(1.0, limit / jnp.sqrt(squares + 1e-06))
    gfilter[...] = back_lag[...].reshape(LANES, BLK).T * scale


def local(outer_gate, inner_gate, value_path, long_filter, skip_gain, cotangent):
    vmem = pl.BlockSpec(memory_space=pltpu.VMEM)
    hbm = pl.BlockSpec(memory_space=pltpu.HBM)
    consts = tables()
    dma = pltpu.SemaphoreType.DMA
    back, back_lag, total = pl.pallas_call(
        conv_kernel,
        out_shape=(
            jax.ShapeDtypeStruct((NCTX, 2 * NAR, BLK), F32),
            jax.ShapeDtypeStruct((NCTX, NAR, BLK), F32),
            jax.ShapeDtypeStruct((8, BLK), F32),
        ),
        in_specs=[hbm] * 10,
        out_specs=(hbm, hbm, vmem),
        scratch_shapes=[pltpu.VMEM((BLK, LANES), BF16)] * 4
        + [pltpu.VMEM((BLK, LANES), F32)]
        + [pltpu.VMEM(c.shape, c.dtype) for c in consts]
        + [
            pltpu.VMEM((NCTX, 2 * NAR, BLK), F32),
            pltpu.VMEM((NCTX, NAR, BLK), F32),
            pltpu.VMEM((NCTX * 2 * NAR, BLK), F32),
            pltpu.VMEM((NCTX * NAR, BLK), F32),
            pltpu.VMEM((NCTX * 2 * NAR, BLK), F32),
            pltpu.VMEM((NCTX * NAR, BLK), F32),
            pltpu.VMEM((NAR // 2, 4 * NCTX, 2 * BLK), F32),
            pltpu.VMEM((3, 8, BLK), F32),
            pltpu.VMEM((3, 8, 8, BLK), F32),
            dma((10,)),
        ]
        + [dma] * 8
        + [dma((3,)), dma((3,)), dma],
        compiler_params=pltpu.CompilerParams(
            collective_id=0, has_side_effects=True, vmem_limit_bytes=VMEM_LIMIT
        ),
    )(outer_gate, inner_gate, value_path, cotangent, long_filter, *consts)
    arr = jax.ShapeDtypeStruct((BLK, LANES), BF16)
    return pl.pallas_call(
        gate_kernel,
        out_shape=(arr, arr, arr, arr, jax.ShapeDtypeStruct((BLK, LANES), F32)),
        in_specs=[hbm] * 4 + [vmem, hbm, hbm, vmem],
        out_specs=(vmem,) * 5,
        scratch_shapes=[pltpu.VMEM((BLK, LANES), BF16)] * 4
        + [
            pltpu.VMEM((NCTX, 2 * NAR, BLK), F32),
            pltpu.VMEM((NCTX, NAR, BLK), F32),
            dma((6,)),
        ],
        compiler_params=pltpu.CompilerParams(vmem_limit_bytes=VMEM_LIMIT),
    )(
        outer_gate, inner_gate, value_path, cotangent, skip_gain.reshape(1, LANES),
        back, back_lag, total,
    )


def solution(mesh):
    big = P("ctx", "ch")
    return jax.shard_map(
        local,
        mesh=mesh,
        in_specs=(big, big, big, big, P("ch"), big),
        out_specs=(big,) * 5,
        check_vma=False,
    )
```

time: 86.7 us -> 69.8 us (0.81)
  the two profiles are of different devices: /device:TPU:1 before, /device:TPU:24 now
where the time goes in v1:
time: 69.8 us; the launch traced here: 69.6 us
  Pallas kernels  69 us (99%)
    pallas_call x1, Pallas kernels, local(): pl.pallas_call(conv_kernel, out_shape=(jax.ShapeDtypeStruct((NCTX, 2 * NA...  65.9 us
    pallas_call x1, Pallas kernels, local(): pl.pallas_call(gate_kernel, out_shape=(arr, arr, arr, arr, jax.ShapeDtype...  3.07 us

profile of v1, /device:TPU:24, one launch (start us, length us, event | category | flops | bytes accessed | tf_op | source)
XLA Modules:
  0.0 69.6 jit_solution(6035339594275472506)
XLA Ops:
  0.6 65.9 %shard_map.146 = (f32[64,16,128]{2,1,0:T(8,128)}, f32[64,8,128]{2,1,0:T(8,128)}, f32[8,128]{1,0:T(8,128)}) custom-call(bf16[128,512]{1,0:T(8,128)(2,1)} %outer_h.3, bf16[128,512]{1,0:T(8,128)(2,1)} %inner_h.3, bf16[128,512]{1,0:T(8,128)(2,1)} %value_h.3, bf16[128,512]{1,0:T(8,128)(2,1)} %cot_h.3, f32[128,512]{1,0:T(8,128)} %filt_h.1, ...), custom_call_target="tpu_custom_call" | custom-call | tf_op jit(solution)/shard_map/pallas_call | solution.py:286
  66.6 3.1 %shard_map.147 = (bf16[128,512]{1,0:T(8,128)(2,1)}, bf16[128,512]{1,0:T(8,128)(2,1)}, bf16[128,512]{1,0:T(8,128)(2,1)}, bf16[128,512]{1,0:T(8,128)(2,1)}, f32[128,512]{1,0:T(8,128)}) custom-call(bf16[128,512]{1,0:T(8,128)(2,1)} %outer_h.3, bf16[128,512]{1,0:T(8,128)(2,1)} %inner_h.3, bf16[128,512]{1,0:T(8,128)(2,1)} %value_h.3, bf16[128,512]{1,0:T(8,128)(2,1)} %cot_h.3, ...), custom_call_target="tpu_custom_call" | custom-call | tf_op jit(solution)/shard_map/pallas_call | solution.py:317

commit v2 on v1

v2 whole, which is shorter than its diff:
```python
import jax
import jax.numpy as jnp
import numpy as np
from jax import lax
from jax.experimental import pallas as pl
from jax.experimental.pallas import tpu as pltpu
from jax.sharding import PartitionSpec as P

F32 = jnp.float32
BF16 = jnp.bfloat16
MESH = pl.DeviceIdType.MESH

NCTX = 64
NCH = 8
VMEM_LIMIT = 60 * 1024 * 1024
BLK = 128
LANES = 512
NAR = LANES // NCTX
HALF = NAR // 2
LN2 = float(np.log(2.0))
DIGITS = 511.0
CODE_MAX = 255.0 * DIGITS + 255.0
STEP = 2.0**-22
TINY = 2.0**-80
FILTER_CODE = (CODE_MAX / 24.0, 28.0)
LAG_CODE = (CODE_MAX / 128.0, 102.0)


def split(x):
    hi = x.astype(BF16)
    lo = (x - hi.astype(F32)).astype(BF16)
    return hi, lo


def tables():
    total = NCTX * BLK
    p = np.arange(NCTX)
    s = np.arange(BLK)
    k = np.arange(NCTX) + 0.25
    a1 = 2 * np.pi * np.outer(k, p) / NCTX
    w1 = np.concatenate([np.cos(a1), -np.sin(a1)], axis=0)
    at = 2 * np.pi * np.outer(k, s) / total
    tw = np.stack([np.cos(at), -np.sin(at)])
    a2 = 2 * np.pi * (np.outer(s, s) % BLK) / BLK
    c, sn = np.cos(a2), np.sin(a2)
    w2 = np.block([[c, -sn], [sn, c]])

    def parts(m):
        hi = m.astype(BF16)
        lo = (m - hi.astype(np.float64)).astype(BF16)
        return hi, lo

    w1h, w1l = parts(w1)
    w1f = np.concatenate([w1h, w1l, w1h], axis=1)
    w1i = np.concatenate([w1h.T, w1l.T, w1h.T], axis=1)
    w2h, w2l = parts(w2)
    w2f = np.stack([w2h, w2l])
    w2i = np.stack([w2h.T, w2l.T])
    return w1f, w1i, tw.astype(np.float32), w2f, w2i


def round13(x):
    c = x * 2049.0
    return c - (c - x)


def pack(a, b, c, log_scale, log_shift):
    code = jnp.round(jnp.log(jnp.abs(c)) * (log_scale / LN2) + log_shift * log_scale)
    code = jnp.clip(code, 0.0, CODE_MAX)
    code = jnp.where(c < 0, -code, code)
    high = jnp.round(code * (1.0 / DIGITS))
    low = code - high * DIGITS

    def word(v, digit):
        v = jnp.where(jnp.abs(v) < TINY, TINY, round13(v))
        return v + v * (digit * STEP)

    return word(a, high), word(b, low)


def unpack(wa, wb, log_scale, log_shift):
    def parts(w):
        v = round13(w)
        digit = jnp.round((w - v) * pl.reciprocal(v * STEP, approx=True))
        return jnp.where(jnp.abs(v) <= TINY, 0.0, v), digit

    a, high = parts(wa)
    b, low = parts(wb)
    code = high * DIGITS + low
    c = jnp.exp2(jnp.abs(code) * (1.0 / log_scale) - log_shift)
    c = jnp.where(code < 0, -c, c)
    return a, b, jnp.where(code == 0, 0.0, c)


def dot(a, b):
    return jnp.dot(a, b, preferred_element_type=F32)


def dot3(x, w_ref):
    hi, lo = split(x)
    wh = w_ref[0]
    return dot(hi, wh) + (dot(hi, w_ref[1]) + dot(lo, wh))


def place(me):
    return lax.div(me, 16), lax.rem(lax.div(me, 2), 8), lax.rem(me, 2)


def peer(me, i):
    x, z, y = place(me)
    k, j = lax.div(i, 8), lax.rem(i, 8)
    dy = 1 - lax.div(k, 4)
    k = lax.rem(k, 4)
    dx = 2 + lax.div(k + 1, 2) * (1 - 2 * lax.rem(k, 2))
    dz = 4 + lax.div(j + 1, 2) * (1 - 2 * lax.rem(j, 2))
    return lax.rem(x + dx, 4) * 16 + lax.rem(z + dz, 8) * 2 + lax.rem(y + dy, 2)


def conv_kernel(
    outer_h, inner_h, value_h, cot_h, filt_h, w1f_h, w1i_h, tw_h, w2f_h, w2i_h,
    back0, back1,
    outer, inner, value, cot, filt, w1f, w1i, tw, w2f, w2i,
    send0, send1, recv0, recv1, ret0, ret1, spec, lags, part, sums,
    load_sem, send_sem, recv_sem, sendr_sem, recvr_sem, sq_send, sq_recv,
):
    me = lax.axis_index("ctx")
    ch = lax.axis_index("ch")

    loads = [
        pltpu.make_async_copy(src, dst, load_sem.at[n])
        for n, (src, dst) in enumerate(
            [
                (inner_h, inner), (value_h, value), (cot_h, cot), (outer_h, outer),
                (filt_h, filt), (w1f_h, w1f), (w1i_h, w1i), (tw_h, tw), (w2f_h, w2f),
                (w2i_h, w2i),
            ]
        )
    ]
    for load in loads:
        load.start()

    barrier = pltpu.get_barrier_semaphore()

    def greet(i, _):
        pl.semaphore_signal(
            barrier, inc=1, device_id={"ctx": peer(me, i)}, device_id_type=MESH
        )
        return 0

    lax.fori_loop(0, NCTX - 1, greet, 0)
    for j in range(1, NCH):
        pl.semaphore_signal(
            barrier, inc=1, device_id={"ch": lax.rem(ch + j, NCH)}, device_id_type=MESH
        )

    for load in loads[:5]:
        load.wait()
    mixed = inner[...].astype(F32) * value[...].astype(F32)
    gconv = cot[...].astype(F32) * outer[...].astype(F32)
    wa, wb = pack(mixed, gconv, filt[...], *FILTER_CODE)
    wa = wa.T.reshape(NCTX, NAR, BLK)
    wb = wb.T.reshape(NCTX, NAR, BLK)
    send0[...] = jnp.concatenate([wa[:, :HALF], wb[:, :HALF]], axis=1)
    send1[...] = jnp.concatenate([wa[:, HALF:], wb[:, HALF:]], axis=1)
    for load in loads[5:]:
        load.wait()

    pl.semaphore_wait(barrier, NCTX - 1 + NCH - 1)

    def spread(src, dst, send_s, recv_s):
        def one(i, _):
            to = peer(me, i)
            pltpu.make_async_remote_copy(
                src_ref=src(to),
                dst_ref=dst(me),
                send_sem=send_s,
                recv_sem=recv_s,
                device_id={"ctx": to},
                device_id_type=MESH,
            ).start()
            return 0

        lax.fori_loop(0, NCTX - 1, one, 0)
        pltpu.make_async_copy(src(me), dst(me), recv_s).start()

    def out_to(n):
        recv = (recv0, recv1)[n]
        send = (send0, send1)[n]
        spread(
            lambda d: send.at[d], lambda d: recv.at[pl.ds(d * 8, 8)],
            send_sem.at[n], recv_sem.at[n],
        )

    out_to(0)
    out_to(1)

    tr, ti = tw[0], tw[1]
    wa, wb = w1f[...], w1i[...]

    def forward(rows):
        hi, lo = split(rows)
        z = dot(wa, jnp.concatenate([hi, hi, lo], axis=0))
        zr, zi = z[:NCTX], z[NCTX:]
        return jnp.concatenate([zr * tr - zi * ti, zr * ti + zi * tr], axis=1)

    def inverse(v):
        vr, vi = v[:, :BLK], v[:, BLK:]
        u = jnp.concatenate([vr * tr + vi * ti, vi * tr - vr * ti], axis=0)
        hi, lo = split(u)
        return dot(wb, jnp.concatenate([hi, hi, lo], axis=0)) * (1.0 / (NCTX * BLK))

    def correlate(a, b):
        ar, ai, br, bi = a[:, :BLK], a[:, BLK:], b[:, :BLK], b[:, BLK:]
        return jnp.concatenate([ar * br + ai * bi, ar * bi - ai * br], axis=1)

    def convolve(a, b):
        ar, ai, br, bi = a[:, :BLK], a[:, BLK:], b[:, :BLK], b[:, BLK:]
        return jnp.concatenate([ar * br - ai * bi, ar * bi + ai * br], axis=1)

    def pieces(v):
        return [v[n * NCTX : (n + 1) * NCTX] for n in range(v.shape[0] // NCTX)]

    def taken(recv, c):
        return unpack(
            recv[pl.ds(c, NCTX, stride=8), :],
            recv[pl.ds(HALF + c, NCTX, stride=8), :],
            *FILTER_CODE,
        )

    def lag_pair(recv):
        def run(n, acc):
            c = 2 * n
            a, b = taken(recv, c), taken(recv, c + 1)
            u = [forward(v) for v in (a[0], b[0], a[1], b[1], a[2], b[2])]
            f = dot3(jnp.concatenate(u, axis=0), w2f)
            spec[n] = f
            m0, m1, g0, g1, _, _ = pieces(f)
            v = dot3(jnp.concatenate([correlate(m0, g0), correlate(m1, g1)], axis=0), w2i)
            for d, part_v in enumerate(pieces(v)):
                lag = inverse(part_v)
                lags[c + d] = lag
                acc = acc + jnp.sum((lag * lag).reshape(NCTX // 8, 8, BLK), axis=0)
            return acc

        return run

    def conv_pair(ret, stride):
        def run(n, carry):
            c = 2 * n
            m0, m1, g0, g1, f0, f1 = pieces(spec[n])
            v = dot3(
                jnp.concatenate(
                    [convolve(f0, m0), convolve(f1, m1), correlate(f0, g0), correlate(f1, g1)],
                    axis=0,
                ),
                w2i,
            )
            y0, y1, b0, b1 = [inverse(p) for p in pieces(v)]
            for d, (y, b) in enumerate([(y0, b0), (y1, b1)]):
                wa, wb = pack(y, b, lags[c + d], *LAG_CODE)
                ret[pl.ds(c + d, NCTX, stride=stride), :] = wa
                ret[pl.ds(HALF + c + d, NCTX, stride=stride), :] = wb
            return carry

        return run

    pltpu.make_async_copy(recv0, recv0, recv_sem.at[0]).wait()
    acc = lax.fori_loop(0, HALF // 2, lag_pair(recv0), jnp.zeros((8, BLK), F32))
    lax.fori_loop(0, HALF // 2, conv_pair(ret0, 8), 0)
    spread(
        lambda d: ret0.at[pl.ds(d * 8, 8)], lambda d: back0.at[d],
        sendr_sem.at[0], recvr_sem.at[0],
    )

    pltpu.make_async_copy(recv1, recv1, recv_sem.at[1]).wait()
    acc = lax.fori_loop(0, HALF // 2, lag_pair(recv1), acc)

    part[...] = acc
    sums[ch] = acc
    for j in range(1, NCH):
        pltpu.make_async_remote_copy(
            src_ref=part,
            dst_ref=sums.at[ch],
            send_sem=sq_send,
            recv_sem=sq_recv,
            device_id={"ch": lax.rem(ch + j, NCH)},
            device_id_type=MESH,
        ).start()
    lax.fori_loop(0, HALF // 2, conv_pair(ret1, 16), 0)
    seven = sums.at[pl.ds(0, NCH - 1)]
    pltpu.make_async_copy(seven, seven, sq_send).wait()
    pltpu.make_async_copy(seven, seven, sq_recv).wait()
    group = jnp.sum(jnp.sum(sums[...], axis=0), axis=0, keepdims=True)
    ret1[pl.ds(8, NCTX, stride=16), :] = jnp.broadcast_to(group, (NCTX, BLK))
    spread(
        lambda d: ret1.at[pl.ds(d * 16, 9)], lambda d: back1.at[d, pl.ds(0, 9)],
        sendr_sem.at[1], recvr_sem.at[1],
    )

    others = pl.ds(0, NCTX - 1)
    for n, ref in enumerate((send0, send1)):
        pltpu.make_async_copy(ref.at[others], ref.at[others], send_sem.at[n]).wait()
    pltpu.make_async_copy(back0.at[others], back0.at[others], sendr_sem.at[0]).wait()
    nine = back1.at[others, pl.ds(0, 9)]
    pltpu.make_async_copy(nine, nine, sendr_sem.at[1]).wait()
    pltpu.make_async_copy(back0, back0, recvr_sem.at[0]).wait()
    nine = back1.at[:, pl.ds(0, 9)]
    pltpu.make_async_copy(nine, nine, recvr_sem.at[1]).wait()


def gate_kernel(
    outer_h, inner_h, value_h, cot_h, skip, back0_h, back1_h,
    hyena, gouter, ginner, gvalue, gfilter,
    outer, inner, value, cot, back0, back1, sem,
):
    loads = [
        pltpu.make_async_copy(src, dst, sem.at[n])
        for n, (src, dst) in enumerate(
            [
                (back0_h, back0), (back1_h, back1), (inner_h, inner), (value_h, value), (outer_h, outer),
                (cot_h, cot),
            ]
        )
    ]
    for load in loads:
        load.start()
    for load in loads:
        load.wait()
    inner_f = inner[...].astype(F32)
    value_f = value[...].astype(F32)
    outer_f = outer[...].astype(F32)
    cot_f = cot[...].astype(F32)
    gain = skip[...]
    b0, b1 = back0[...], back1[...]
    wa = jnp.concatenate([b0[:, :HALF], b1[:, :HALF]], axis=1).reshape(LANES, BLK).T
    wb = jnp.concatenate([b0[:, HALF:], b1[:, HALF : 2 * HALF]], axis=1).reshape(LANES, BLK).T
    conv, corr, lag = unpack(wa, wb, *LAG_CODE)
    base = conv + gain * (inner_f * value_f)
    hyena[...] = (outer_f * base).astype(BF16)
    gouter[...] = (cot_f * base).astype(BF16)
    gmixed = corr + gain * (cot_f * outer_f)
    ginner[...] = (gmixed * value_f).astype(BF16)
    gvalue[...] = (gmixed * inner_f).astype(BF16)
    squares = jnp.sum(jnp.sum(b1[:, 8, :], axis=0, keepdims=True), axis=1, keepdims=True)
    limit = float(NCTX * BLK) * float(np.sqrt(LANES * NCH))
    scale = jnp.minimum(1.0, limit / jnp.sqrt(squares + 1e-06))
    gfilter[...] = lag * scale


def local(outer_gate, inner_gate, value_path, long_filter, skip_gain, cotangent):
    vmem = pl.BlockSpec(memory_space=pltpu.VMEM)
    hbm = pl.BlockSpec(memory_space=pltpu.HBM)
    consts = tables()
    dma = pltpu.SemaphoreType.DMA
    back0, back1 = pl.pallas_call(
        conv_kernel,
        out_shape=(
            jax.ShapeDtypeStruct((NCTX, 8, BLK), F32),
            jax.ShapeDtypeStruct((NCTX, 16, BLK), F32),
        ),
        in_specs=[hbm] * 10,
        out_specs=(hbm, hbm),
        scratch_shapes=[pltpu.VMEM((BLK, LANES), BF16)] * 4
        + [pltpu.VMEM((BLK, LANES), F32)]
        + [pltpu.VMEM(c.shape, c.dtype) for c in consts]
        + [
            pltpu.VMEM((NCTX, 8, BLK), F32),
            pltpu.VMEM((NCTX, 8, BLK), F32),
            pltpu.VMEM((NCTX * 8, BLK), F32),
            pltpu.VMEM((NCTX * 8, BLK), F32),
            pltpu.VMEM((NCTX * 8, BLK), F32),
            pltpu.VMEM((NCTX * 16, BLK), F32),
            pltpu.VMEM((HALF // 2, 6 * NCTX, 2 * BLK), F32),
            pltpu.VMEM((HALF, NCTX, BLK), F32),
            pltpu.VMEM((8, BLK), F32),
            pltpu.VMEM((NCH, 8, BLK), F32),
            dma((10,)),
        ]
        + [dma((2,))] * 4
        + [dma, dma],
        compiler_params=pltpu.CompilerParams(
            collective_id=0, has_side_effects=True, vmem_limit_bytes=VMEM_LIMIT
        ),
    )(outer_gate, inner_gate, value_path, cotangent, long_filter, *consts)
    arr = jax.ShapeDtypeStruct((BLK, LANES), BF16)
    return pl.pallas_call(
        gate_kernel,
        out_shape=(arr, arr, arr, arr, jax.ShapeDtypeStruct((BLK, LANES), F32)),
        in_specs=[hbm] * 4 + [vmem, hbm, hbm],
        out_specs=(vmem,) * 5,
        scratch_shapes=[pltpu.VMEM((BLK, LANES), BF16)] * 4
        + [
            pltpu.VMEM((NCTX, 8, BLK), F32),
            pltpu.VMEM((NCTX, 16, BLK), F32),
            dma((6,)),
        ],
        compiler_params=pltpu.CompilerParams(vmem_limit_bytes=VMEM_LIMIT),
    )(
        outer_gate, inner_gate, value_path, cotangent, skip_gain.reshape(1, LANES),
        back0, back1,
    )


def solution(mesh):
    big = P("ctx", "ch")
    return jax.shard_map(
        local,
        mesh=mesh,
        in_specs=(big, big, big, big, P("ch"), big),
        out_specs=(big,) * 5,
        check_vma=False,
    )
```

time: 69.8 us -> 57.3 us (0.82)
  the two profiles are of different devices: /device:TPU:24 before, /device:TPU:1 now
where the time goes in v2:
time: 57.3 us; the launch traced here: 57.1 us
  Pallas kernels  56.5 us (99%)
  between operations  0.64 us (1%)
    pallas_call x1, Pallas kernels, local(): pl.pallas_call(conv_kernel, out_shape=(jax.ShapeDtypeStruct((NCTX, 8, BLK...  53.2 us
    pallas_call x1, Pallas kernels, local(): pl.pallas_call(gate_kernel, out_shape=(arr, arr, arr, arr, jax.ShapeDtype...  3.27 us

profile of v2, /device:TPU:1, one launch (start us, length us, event | category | flops | bytes accessed | tf_op | source)
XLA Modules:
  0.0 57.1 jit_solution(3853235301029962848)
XLA Ops:
  0.6 53.2 %shard_map.146 = (f32[64,8,128]{2,1,0:T(8,128)}, f32[64,16,128]{2,1,0:T(8,128)}) custom-call(bf16[128,512]{1,0:T(8,128)(2,1)} %outer_h.3, bf16[128,512]{1,0:T(8,128)(2,1)} %inner_h.3, bf16[128,512]{1,0:T(8,128)(2,1)} %value_h.3, bf16[128,512]{1,0:T(8,128)(2,1)} %cot_h.3, f32[128,512]{1,0:T(8,128)} %filt_h.1, bf16[128,192]{1,0:T(8,128)(2,1)} %constant.10.clone.w1f_h, ...), custom_call_target="tpu_custom_call" | custom-call | tf_op jit(solution)/shard_map/pallas_call | solution.py:355
  53.8 3.3 %shard_map.147 = (bf16[128,512]{1,0:T(8,128)(2,1)}, bf16[128,512]{1,0:T(8,128)(2,1)}, bf16[128,512]{1,0:T(8,128)(2,1)}, bf16[128,512]{1,0:T(8,128)(2,1)}, f32[128,512]{1,0:T(8,128)}) custom-call(bf16[128,512]{1,0:T(8,128)(2,1)} %outer_h.3, bf16[128,512]{1,0:T(8,128)(2,1)} %inner_h.3, bf16[128,512]{1,0:T(8,128)(2,1)} %value_h.3, bf16[128,512]{1,0:T(8,128)(2,1)} %cot_h.3, ...), custom_call_target="tpu_custom_call" | custom-call | tf_op jit(solution)/shard_map/pallas_call | solution.py:386

commit v3 on v2

--- a/solution.py
+++ b/solution.py
@@ -116,6 +116,17 @@
     return lax.rem(x + dx, 4) * 16 + lax.rem(z + dz, 8) * 2 + lax.rem(y + dy, 2)
 
 
+def ranked(me, i):
+    x, z, y = place(me)
+    g, r = lax.div(i, 16), lax.rem(i, 16)
+    dy = 1 - lax.div(r, 8)
+    r = lax.rem(r, 8)
+    k, j = lax.div(r, 2), lax.rem(r, 2)
+    dx = 2 + lax.div(k + 1, 2) * (1 - 2 * lax.rem(k, 2))
+    low = lax.rem(z + j, 2)
+    return lax.rem(x + dx, 4) * 16 + (2 * g + low) * 2 + lax.rem(y + dy, 2)
+
+
 def conv_kernel(
     outer_h, inner_h, value_h, cot_h, filt_h, w1f_h, w1i_h, tw_h, w2f_h, w2i_h,
     back0, back1,
@@ -147,7 +158,7 @@
         )
         return 0
 
-    lax.fori_loop(0, NCTX - 1, greet, 0)
+    lax.fori_loop(0, NCTX - 1, greet, 0, unroll=7)
     for j in range(1, NCH):
         pl.semaphore_signal(
             barrier, inc=1, device_id={"ch": lax.rem(ch + j, NCH)}, device_id_type=MESH
@@ -180,8 +191,29 @@
             ).start()
             return 0
 
-        lax.fori_loop(0, NCTX - 1, one, 0)
+        lax.fori_loop(0, NCTX - 1, one, 0, unroll=7)
         pltpu.make_async_copy(src(me), dst(me), recv_s).start()
+
+    def spread_ranked(src, dst, send_s, recv_s, first, last):
+        def one(i, _):
+            to = ranked(me, i)
+
+            @pl.when(to != me)
+            def _():
+                pltpu.make_async_remote_copy(
+                    src_ref=src(to),
+                    dst_ref=dst(me),
+                    send_sem=send_s,
+                    recv_sem=recv_s,
+                    device_id={"ctx": to},
+                    device_id_type=MESH,
+                ).start()
+
+            return 0
+
+        lax.fori_loop(first, last, one, 0, unroll=4)
+        if first == 0:
+            pltpu.make_async_copy(src(me), dst(me), recv_s).start()
 
     def out_to(n):
         recv = (recv0, recv1)[n]
@@ -267,9 +299,9 @@
     pltpu.make_async_copy(recv0, recv0, recv_sem.at[0]).wait()
     acc = lax.fori_loop(0, HALF // 2, lag_pair(recv0), jnp.zeros((8, BLK), F32))
     lax.fori_loop(0, HALF // 2, conv_pair(ret0, 8), 0)
-    spread(
+    spread_ranked(
         lambda d: ret0.at[pl.ds(d * 8, 8)], lambda d: back0.at[d],
-        sendr_sem.at[0], recvr_sem.at[0],
+        sendr_sem.at[0], recvr_sem.at[0], 0, 64
     )
 
     pltpu.make_async_copy(recv1, recv1, recv_sem.at[1]).wait()
@@ -292,9 +324,9 @@
     pltpu.make_async_copy(seven, seven, sq_recv).wait()
     group = jnp.sum(jnp.sum(sums[...], axis=0), axis=0, keepdims=True)
     ret1[pl.ds(8, NCTX, stride=16), :] = jnp.broadcast_to(group, (NCTX, BLK))
-    spread(
+    spread_ranked(
         lambda d: ret1.at[pl.ds(d * 16, 9)], lambda d: back1.at[d, pl.ds(0, 9)],
-        sendr_sem.at[1], recvr_sem.at[1],
+        sendr_sem.at[1], recvr_sem.at[1], 0, 64,
     )
 
     others = pl.ds(0, NCTX - 1)
@@ -309,16 +341,16 @@
 
 
 def gate_kernel(
-    outer_h, inner_h, value_h, cot_h, skip, back0_h, back1_h,
+    outer_h, inner_h, value_h, cot_h, skip_h, back0_h, back1_h,
     hyena, gouter, ginner, gvalue, gfilter,
-    outer, inner, value, cot, back0, back1, sem,
+    outer, inner, value, cot, back0, back1, skip, sem,
 ):
     loads = [
         pltpu.make_async_copy(src, dst, sem.at[n])
         for n, (src, dst) in enumerate(
             [
                 (back0_h, back0), (back1_h, back1), (inner_h, inner), (value_h, value), (outer_h, outer),
-                (cot_h, cot),
+                (cot_h, cot), (skip_h, skip),
             ]
         )
     ]
@@ -386,13 +418,14 @@
     return pl.pallas_call(
         gate_kernel,
         out_shape=(arr, arr, arr, arr, jax.ShapeDtypeStruct((BLK, LANES), F32)),
-        in_specs=[hbm] * 4 + [vmem, hbm, hbm],
+        in_specs=[hbm] * 7,
         out_specs=(vmem,) * 5,
         scratch_shapes=[pltpu.VMEM((BLK, LANES), BF16)] * 4
         + [
             pltpu.VMEM((NCTX, 8, BLK), F32),
             pltpu.VMEM((NCTX, 16, BLK), F32),
-            dma((6,)),
+            pltpu.VMEM((1, LANES), F32),
+            dma((7,)),
         ],
         compiler_params=pltpu.CompilerParams(vmem_limit_bytes=VMEM_LIMIT),
     )(

time: 57.3 us -> 53.8 us (0.939); the launches traced: 57.1 us -> 52.9 us
  Pallas kernels: 56.5 us -> 52.3 us
    pallas_call x1, Pallas kernels: 53.2 us -> 49.7 us  [local(): pl.pallas_call(conv_kernel, out_shape=(jax.ShapeDtypeStruct((NCTX, 8, BLK...]
    pallas_call x1, Pallas kernels: 3.27 us -> 2.6 us  [local(): pl.pallas_call(gate_kernel, out_shape=(arr, arr, arr, arr, jax.ShapeDtype...]
where the time goes in v3:
time: 53.8 us; the launch traced here: 52.9 us
  Pallas kernels  52.3 us (97%)
  between operations  0.64 us (1%)
    pallas_call x1, Pallas kernels, local(): pl.pallas_call(conv_kernel, out_shape=(jax.ShapeDtypeStruct((NCTX, 8, BLK...  49.7 us
    pallas_call x1, Pallas kernels, local(): pl.pallas_call(gate_kernel, out_shape=(arr, arr, arr, arr, jax.ShapeDtype...  2.6 us

profile of v3, /device:TPU:1, one launch (start us, length us, event | category | flops | bytes accessed | tf_op | source)
XLA Modules:
  0.0 52.9 jit_solution(11661580011425876327)
XLA Ops:
  0.6 49.7 %shard_map.146 = (f32[64,8,128]{2,1,0:T(8,128)}, f32[64,16,128]{2,1,0:T(8,128)}) custom-call(bf16[128,512]{1,0:T(8,128)(2,1)} %outer_h.3, bf16[128,512]{1,0:T(8,128)(2,1)} %inner_h.3, bf16[128,512]{1,0:T(8,128)(2,1)} %value_h.3, bf16[128,512]{1,0:T(8,128)(2,1)} %cot_h.3, f32[128,512]{1,0:T(8,128)} %filt_h.1, bf16[128,192]{1,0:T(8,128)(2,1)} %constant.10.clone.w1f_h, ...), custom_call_target="tpu_custom_call" | custom-call | tf_op jit(solution)/shard_map/pallas_call | solution.py:387
  50.3 2.6 %shard_map.147 = (bf16[128,512]{1,0:T(8,128)(2,1)}, bf16[128,512]{1,0:T(8,128)(2,1)}, bf16[128,512]{1,0:T(8,128)(2,1)}, bf16[128,512]{1,0:T(8,128)(2,1)}, f32[128,512]{1,0:T(8,128)}) custom-call(bf16[128,512]{1,0:T(8,128)(2,1)} %outer_h.3, bf16[128,512]{1,0:T(8,128)(2,1)} %inner_h.3, bf16[128,512]{1,0:T(8,128)(2,1)} %value_h.3, bf16[128,512]{1,0:T(8,128)(2,1)} %cot_h.3, ...), custom_call_target="tpu_custom_call" | custom-call | tf_op jit(solution)/shard_map/pallas_call | solution.py:418

commit v4 on v3

--- a/solution.py
+++ b/solution.py
@@ -119,8 +119,8 @@
 def ranked(me, i):
     x, z, y = place(me)
     g, r = lax.div(i, 16), lax.rem(i, 16)
-    dy = 1 - lax.div(r, 8)
-    r = lax.rem(r, 8)
+    dy = 1 - lax.rem(r, 2)
+    r = lax.div(r, 2)
     k, j = lax.div(r, 2), lax.rem(r, 2)
     dx = 2 + lax.div(k + 1, 2) * (1 - 2 * lax.rem(k, 2))
     low = lax.rem(z + j, 2)
@@ -147,7 +147,7 @@
             ]
         )
     ]
-    for load in loads:
+    for load in loads[:5]:
         load.start()
 
     barrier = pltpu.get_barrier_semaphore()
@@ -163,6 +163,9 @@
         pl.semaphore_signal(
             barrier, inc=1, device_id={"ch": lax.rem(ch + j, NCH)}, device_id_type=MESH
         )
+
+    for load in loads[5:]:
+        load.start()
 
     for load in loads[:5]:
         load.wait()
@@ -229,17 +232,26 @@
     tr, ti = tw[0], tw[1]
     wa, wb = w1f[...], w1i[...]
 
-    def forward(rows):
-        hi, lo = split(rows)
+    def forward(rows0, rows1):
+        h0, l0 = split(rows0)
+        h1, l1 = split(rows1)
+        hi = jnp.concatenate([h0, h1], axis=1)
+        lo = jnp.concatenate([l0, l1], axis=1)
         z = dot(wa, jnp.concatenate([hi, hi, lo], axis=0))
-        zr, zi = z[:NCTX], z[NCTX:]
-        return jnp.concatenate([zr * tr - zi * ti, zr * ti + zi * tr], axis=1)
-
-    def inverse(v):
-        vr, vi = v[:, :BLK], v[:, BLK:]
-        u = jnp.concatenate([vr * tr + vi * ti, vi * tr - vr * ti], axis=0)
-        hi, lo = split(u)
-        return dot(wb, jnp.concatenate([hi, hi, lo], axis=0)) * (1.0 / (NCTX * BLK))
+        out = []
+        for d in (0, 1):
+            zr, zi = z[:NCTX, d * BLK : (d + 1) * BLK], z[NCTX:, d * BLK : (d + 1) * BLK]
+            out.append(jnp.concatenate([zr * tr - zi * ti, zr * ti + zi * tr], axis=1))
+        return out
+
+    def inverse(v0, v1):
+        us = []
+        for v in (v0, v1):
+            vr, vi = v[:, :BLK], v[:, BLK:]
+            us.append(jnp.concatenate([vr * tr + vi * ti, vi * tr - vr * ti], axis=0))
+        hi, lo = split(jnp.concatenate(us, axis=1))
+        y = dot(wb, jnp.concatenate([hi, hi, lo], axis=0)) * (1.0 / (NCTX * BLK))
+        return y[:, :BLK], y[:, BLK:]
 
     def correlate(a, b):
         ar, ai, br, bi = a[:, :BLK], a[:, BLK:], b[:, :BLK], b[:, BLK:]
@@ -251,6 +263,8 @@
 
     def pieces(v):
         return [v[n * NCTX : (n + 1) * NCTX] for n in range(v.shape[0] // NCTX)]
+
+    tiles = pl.ds(0, NCTX * 8)
 
     def taken(recv, c):
         return unpack(
@@ -259,53 +273,50 @@
             *FILTER_CODE,
         )
 
-    def lag_pair(recv):
-        def run(n, acc):
-            c = 2 * n
+    def lag_half(recv, acc):
+        us = []
+        for c in range(0, HALF, 2):
             a, b = taken(recv, c), taken(recv, c + 1)
-            u = [forward(v) for v in (a[0], b[0], a[1], b[1], a[2], b[2])]
-            f = dot3(jnp.concatenate(u, axis=0), w2f)
-            spec[n] = f
-            m0, m1, g0, g1, _, _ = pieces(f)
-            v = dot3(jnp.concatenate([correlate(m0, g0), correlate(m1, g1)], axis=0), w2i)
-            for d, part_v in enumerate(pieces(v)):
-                lag = inverse(part_v)
+            us += forward(a[0], b[0]) + forward(a[1], b[1]) + forward(a[2], b[2])
+        f = dot3(jnp.concatenate(us, axis=0), w2f)
+        spec[...] = f
+        f = pieces(f)
+        prods = []
+        for c in range(0, HALF, 2):
+            m0, m1, g0, g1 = f[3 * c : 3 * c + 4]
+            prods += [correlate(m0, g0), correlate(m1, g1)]
+        v = pieces(dot3(jnp.concatenate(prods, axis=0), w2i))
+        for c in range(0, HALF, 2):
+            for d, lag in enumerate(inverse(v[c], v[c + 1])):
                 lags[c + d] = lag
                 acc = acc + jnp.sum((lag * lag).reshape(NCTX // 8, 8, BLK), axis=0)
-            return acc
-
-        return run
-
-    def conv_pair(ret, stride):
-        def run(n, carry):
-            c = 2 * n
-            m0, m1, g0, g1, f0, f1 = pieces(spec[n])
-            v = dot3(
-                jnp.concatenate(
-                    [convolve(f0, m0), convolve(f1, m1), correlate(f0, g0), correlate(f1, g1)],
-                    axis=0,
-                ),
-                w2i,
-            )
-            y0, y1, b0, b1 = [inverse(p) for p in pieces(v)]
-            for d, (y, b) in enumerate([(y0, b0), (y1, b1)]):
-                wa, wb = pack(y, b, lags[c + d], *LAG_CODE)
+        return acc
+
+    def conv_half(ret, stride):
+        f = pieces(spec[...])
+        prods = []
+        for c in range(0, HALF, 2):
+            m0, m1, g0, g1, f0, f1 = f[3 * c : 3 * c + 6]
+            prods += [convolve(f0, m0), convolve(f1, m1), correlate(f0, g0), correlate(f1, g1)]
+        v = pieces(dot3(jnp.concatenate(prods, axis=0), w2i))
+        for c in range(0, HALF, 2):
+            ys = inverse(v[2 * c], v[2 * c + 1])
+            bs = inverse(v[2 * c + 2], v[2 * c + 3])
+            for d in (0, 1):
+                wa, wb = pack(ys[d], bs[d], lags[c + d], *LAG_CODE)
                 ret[pl.ds(c + d, NCTX, stride=stride), :] = wa
                 ret[pl.ds(HALF + c + d, NCTX, stride=stride), :] = wb
-            return carry
-
-        return run
-
-    pltpu.make_async_copy(recv0, recv0, recv_sem.at[0]).wait()
-    acc = lax.fori_loop(0, HALF // 2, lag_pair(recv0), jnp.zeros((8, BLK), F32))
-    lax.fori_loop(0, HALF // 2, conv_pair(ret0, 8), 0)
+
+    pltpu.make_async_copy(recv0.at[tiles], recv0.at[tiles], recv_sem.at[0]).wait()
+    acc = lag_half(recv0, jnp.zeros((8, BLK), F32))
+    conv_half(ret0, 8)
     spread_ranked(
         lambda d: ret0.at[pl.ds(d * 8, 8)], lambda d: back0.at[d],
         sendr_sem.at[0], recvr_sem.at[0], 0, 64
     )
 
-    pltpu.make_async_copy(recv1, recv1, recv_sem.at[1]).wait()
-    acc = lax.fori_loop(0, HALF // 2, lag_pair(recv1), acc)
+    pltpu.make_async_copy(recv1.at[tiles], recv1.at[tiles], recv_sem.at[1]).wait()
+    acc = lag_half(recv1, acc)
 
     part[...] = acc
     sums[ch] = acc
@@ -318,7 +329,7 @@
             device_id={"ch": lax.rem(ch + j, NCH)},
             device_id_type=MESH,
         ).start()
-    lax.fori_loop(0, HALF // 2, conv_pair(ret1, 16), 0)
+    conv_half(ret1, 16)
     seven = sums.at[pl.ds(0, NCH - 1)]
     pltpu.make_async_copy(seven, seven, sq_send).wait()
     pltpu.make_async_copy(seven, seven, sq_recv).wait()
@@ -398,11 +409,11 @@
         + [
             pltpu.VMEM((NCTX, 8, BLK), F32),
             pltpu.VMEM((NCTX, 8, BLK), F32),
-            pltpu.VMEM((NCTX * 8, BLK), F32),
-            pltpu.VMEM((NCTX * 8, BLK), F32),
-            pltpu.VMEM((NCTX * 8, BLK), F32),
-            pltpu.VMEM((NCTX * 16, BLK), F32),
-            pltpu.VMEM((HALF // 2, 6 * NCTX, 2 * BLK), F32),
+            pltpu.VMEM((NCTX * 8 + 8, BLK), F32),
+            pltpu.VMEM((NCTX * 8 + 8, BLK), F32),
+            pltpu.VMEM((NCTX * 8 + 8, BLK), F32),
+            pltpu.VMEM((NCTX * 16 + 16, BLK), F32),
+            pltpu.VMEM((3 * HALF * NCTX, 2 * BLK), F32),
             pltpu.VMEM((HALF, NCTX, BLK), F32),
             pltpu.VMEM((8, BLK), F32),
             pltpu.VMEM((NCH, 8, BLK), F32),

time: 53.8 us -> 53.3 us (level)
  the two profiles are of different devices: /device:TPU:1 before, /device:TPU:16 now
where the time goes in v4:
time: 53.3 us; the launch traced here: 53.1 us
  Pallas kernels  52.4 us (98%)
  between operations  0.64 us (1%)
    pallas_call x1, Pallas kernels, local(): pl.pallas_call(conv_kernel, out_shape=(jax.ShapeDtypeStruct((NCTX, 8, BLK...  49.9 us
    pallas_call x1, Pallas kernels, local(): pl.pallas_call(gate_kernel, out_shape=(arr, arr, arr, arr, jax.ShapeDtype...  2.6 us

profile of v4, /device:TPU:16, one launch (start us, length us, event | category | flops | bytes accessed | tf_op | source)
XLA Modules:
  0.0 53.1 jit_solution(98241175936091922)
XLA Ops:
  0.6 49.9 %shard_map.146 = (f32[64,8,128]{2,1,0:T(8,128)}, f32[64,16,128]{2,1,0:T(8,128)}) custom-call(bf16[128,512]{1,0:T(8,128)(2,1)} %outer_h.3, bf16[128,512]{1,0:T(8,128)(2,1)} %inner_h.3, bf16[128,512]{1,0:T(8,128)(2,1)} %value_h.3, bf16[128,512]{1,0:T(8,128)(2,1)} %cot_h.3, f32[128,512]{1,0:T(8,128)} %filt_h.1, bf16[128,192]{1,0:T(8,128)(2,1)} %constant.10.clone.w1f_h, ...), custom_call_target="tpu_custom_call" | custom-call | tf_op jit(solution)/shard_map/pallas_call | solution.py:398
  50.5 2.6 %shard_map.147 = (bf16[128,512]{1,0:T(8,128)(2,1)}, bf16[128,512]{1,0:T(8,128)(2,1)}, bf16[128,512]{1,0:T(8,128)(2,1)}, bf16[128,512]{1,0:T(8,128)(2,1)}, f32[128,512]{1,0:T(8,128)}) custom-call(bf16[128,512]{1,0:T(8,128)(2,1)} %outer_h.3, bf16[128,512]{1,0:T(8,128)(2,1)} %inner_h.3, bf16[128,512]{1,0:T(8,128)(2,1)} %value_h.3, bf16[128,512]{1,0:T(8,128)(2,1)} %cot_h.3, ...), custom_call_target="tpu_custom_call" | custom-call | tf_op jit(solution)/shard_map/pallas_call | solution.py:429
